TPU v7x, 32 devices: a whole 2x2x4 slice. The times are simulated.
32 devices in a mesh: parts: 2 (over y), frame: 8 (over z, x), freq: 2 (over core).
Axes of the slice: x: 2, y: 2, z: 4, core: 2. Of those that a mesh axis runs over, the one named last changes fastest.
Arguments:
- spectrogram: bfloat16 [2048, 8192], P('freq', ('parts', 'frame')), parts along dimension 1, may hold values from 0.049804688 to 5
- templates: float32 [4096, 512], P(('parts', 'freq'), 'frame'), parts along dimension 0, may hold values from 0.1 to 2
- activations: float32 [512, 8192], P(None, ('parts', 'frame')), parts along dimension 1, may hold values from 0.001 to 0.03
- score_mask: int32 [512, 64], P(None, ('parts', 'frame')), parts along dimension 1, may hold values from 0 to 1, as said below
Outputs:
- templates_new: float32 [4096, 512], P(('parts', 'freq'), 'frame'), parts along dimension 0
- activations_new: float32 [512, 8192], P(None, ('parts', 'frame')), parts along dimension 1
There are 2 independent parts, one for each index of `parts`. A program takes and returns all parts, laid end to end along the dimension named above; each array names one. Nothing has to cross between parts.
Inputs may be any that keep to these rules, and one draw needn't show every extreme that they name: `score_mask`: 0/1 values.
All inputs are finite; a program needn't handle non-finite values.
Results may differ from a plain program's by a relative error of at most 0.00052.
Values may be sent and summed in bfloat16 or wider, within the bound.
A program may use at most 64 MiB of HBM per device.

v0:
```python
import jax
import jax.numpy as jnp
from jax import lax
from jax.sharding import PartitionSpec as P

BLOCK = 128


def shards(spectrogram, templates, activations, score_mask):
    allowed = jnp.repeat(score_mask.astype(jnp.float32), BLOCK, axis=1)
    acts = activations * allowed
    temps = templates
    note_cols = temps.shape[1]
    h_bf = acts.astype(jnp.bfloat16)
    whole = lax.all_gather(temps.astype(jnp.bfloat16), "frame", axis=1, tiled=True)
    approx = jnp.dot(whole, h_bf, preferred_element_type=jnp.float32).astype(jnp.bfloat16)
    numer_h = jnp.einsum("fk,fn->kn", whole, spectrogram, preferred_element_type=jnp.float32)
    denom_h = jnp.einsum("fk,fn->kn", whole, approx, preferred_element_type=jnp.float32)
    numer_h, denom_h = lax.psum((numer_h, denom_h), "freq")
    acts = allowed * acts * numer_h / (denom_h + 1e-06)
    h_new = acts.astype(jnp.bfloat16)
    numer_w = lax.psum_scatter(
        jnp.einsum("kn,fn->kf", h_new, spectrogram, preferred_element_type=jnp.float32),
        "frame",
        scatter_dimension=0,
        tiled=True,
    ).T
    gram_local = jnp.einsum("kn,jn->kj", h_new, h_new, preferred_element_type=jnp.float32)
    gram = lax.psum(gram_local, "frame")
    own_cols = lax.dynamic_slice_in_dim(gram, lax.axis_index("frame") * note_cols, note_cols, 1)
    denom_w = jnp.dot(whole.astype(jnp.float32), own_cols, precision=lax.Precision.HIGHEST)
    temps = temps * numer_w / (denom_w + 1e-06)
    return (temps, acts)


def solution(mesh):
    return jax.shard_map(
        shards,
        mesh=mesh,
        in_specs=(
            P("freq", ("parts", "frame")),
            P(("parts", "freq"), "frame"),
            P(None, ("parts", "frame")),
            P(None, ("parts", "frame")),
        ),
        out_specs=(P(("parts", "freq"), "frame"), P(None, ("parts", "frame"))),
        check_vma=False,
    )
```

profile of v0, /device:TPU:0, one launch (start us, length us, event | category | flops | bytes accessed | tf_op | source)
XLA Modules:
  0.0 244.3 jit_solution(12828209458879609259)
XLA Ops:
  7.2 0.0 copy-start
  7.2 0.0 all-gather.2.cloned.1.call-start
  7.2 1.7 convert_element_type.18
  8.9 0.0 all-gather.2.cloned.1.call-update
  8.9 0.0 all-reduce.6.cloned.1.call-start
  9.0 0.7 convert_element_type.17
  9.7 0.1 copy.6
  9.9 0.0 copy-start.2
  9.9 43.7 %all-gather.2.cloned.1.call-done = bf16[1024,512]{0,1:T(8,128)(2,1)} async-done(((bf16[1024,64]{0,1:T(8,128)(2,1)}), bf16[1024,512]{0,1:T(8,128)(2,1)}) %all-gather.2.cloned.1.call-update) | async-done | bytes 1048592 | tf_op jit(solution)/shard_map/all_gather | solution.py:15
  53.6 0.0 copy-done
  53.6 2.9 %fusion.13 = f32[512,512]{1,0:T(8,128)} fusion(bf16[1024,512]{0,1:T(8,128)(2,1)} %all-gather.2.cloned.1.call-done, bf16[1024,512]{1,0:T(8,128)(2,1)S(1)} %copy-done), kind=kOutput, calls=%fused_computation.17 | convolution fusion | flops 536870912 | bytes 3145728 | tf_op jit(solution)/shard_map/fk,fn->kn/dot_general | solution.py:17
  56.5 0.6 broadcast_in_dim.3
  57.1 0.0 copy-done.2
  57.1 3.9 %convolution_bitcast_fusion = f32[512,512]{1,0:T(8,128)} fusion(bf16[1024,512]{0,1:T(8,128)(2,1)} %all-gather.2.cloned.1.call-done, f32[512,512]{1,0:T(8,128)S(1)} %copy-done.2, f32[64,8,4,128]{3,2,1,0:T(4,128)S(1)} %bitcast.30), kind=kOutput, calls=%fused_computation.1 | convolution fusion | flops 1074790400 | bytes 4194304 | tf_op jit(solution)/shard_map/fk,fn->kn/dot_general | solution.py:18
  61.0 0.0 all-reduce.6.cloned.1.call-update
  61.0 0.0 all-reduce.4.cloned.1.call-start
  61.1 20.2 %all-reduce.6.cloned.1.call-done = (f32[512,512]{1,0:T(8,128)}, f32[512,512]{1,0:T(8,128)}) async-done(((f32[512,512]{1,0:T(8,128)}, f32[512,512]{1,0:T(8,128)}), (f32[512,512]{1,0:T(8,128)}, f32[512,512]{1,0:T(8,128)})) %all-reduce.6.cloned.1.call-update) | async-done | bytes 2097168 | tf_op jit(solution)/shard_map/psum | solution.py:19
  81.2 2.4 fusion.3
  83.6 0.0 copy-start.1
  83.6 1.4 fusion.8
  85.0 0.0 all-reduce.4.cloned.1.call-update
  85.1 0.0 reduce-scatter.2.cloned.1.call-start
  85.1 2.1 fusion.10
  87.2 0.0 copy-done.1
  87.2 0.0 copy-start.3
  87.2 0.0 copy-start.4
  87.2 0.0 reduce-scatter.2.cloned.1.call-update
  87.2 77.3 %all-reduce.4.cloned.1.call-done = f32[512,512]{1,0:T(8,128)} async-done(((f32[512,512]{1,0:T(8,128)}), f32[512,512]{1,0:T(8,128)}) %all-reduce.4.cloned.1.call-update) | async-done | bytes 1048592 | tf_op jit(solution)/shard_map/psum | solution.py:29
  164.5 70.7 %reduce-scatter.2.cloned.1.call-done = f32[64,1024]{1,0:T(8,128)} async-done(((f32[512,1024]{1,0:T(8,128)}), f32[64,1024]{1,0:T(8,128)}) %reduce-scatter.2.cloned.1.call-update) | async-done | bytes 262160 | tf_op jit(solution)/shard_map/reduce_scatter | solution.py:22
  235.2 0.0 copy-done.3
  235.2 0.0 copy-done.4
  235.2 2.6 %fusion.1 = f32[1024,64]{0,1:T(8,128)} fusion(bf16[1024,512]{0,1:T(8,128)(2,1)S(1)} %copy-done.3, f32[1024,64]{0,1:T(8,128)S(1)} %copy-done.4, f32[64,1024]{1,0:T(8,128)} %reduce-scatter.2.cloned.1.call-done, f32[512,512]{1,0:T(8,128)} %all-reduce.4.cloned.1.call-done, s32[]{:T(128)S(6)} %select_n.3), kind=kOutput, calls=%fused_computation.4 | convolution fusion | flops 402849792 | bytes 2097156 | tf_op jit(solution)/shard_map/dot_general | solution.py:31
Async XLA Ops:
  7.2 46.4 %copy-start = (bf16[1024,512]{1,0:T(8,128)(2,1)S(1)}, bf16[1024,512]{1,0:T(8,128)(2,1)}, u32[]{:S(2)}) copy-start(bf16[1024,512]{1,0:T(8,128)(2,1)} %param.4) | copy-start | bytes 3145732
  7.2 46.4 %all-gather.2.cloned.1.call-start = ((), (), s32[]{:S(2)}) async-start(), calls=%async_computation.1 | async-start | bytes 1179648 | tf_op jit(solution)/shard_map/all_gather | solution.py:15
  8.9 72.3 %all-reduce.6.cloned.1.call-start = ((), (), s32[]{:S(2)}) async-start(), calls=%async_computation.4 | async-start | bytes 4194304 | tf_op jit(solution)/shard_map/psum | solution.py:19
  9.9 47.2 %copy-start.2 = (f32[512,512]{1,0:T(8,128)S(1)}, f32[512,512]{1,0:T(8,128)}, u32[]{:S(2)}) copy-start(f32[512,512]{1,0:T(8,128)} %param.6) | copy-start | bytes 3145732
  61.0 103.5 %all-reduce.4.cloned.1.call-start = ((), (), s32[]{:S(2)}) async-start(), calls=%async_computation.3 | async-start | bytes 2097152 | tf_op jit(solution)/shard_map/psum | solution.py:29
  83.6 3.6 %copy-start.1 = (f32[512,512]{1,0:T(8,128)}, f32[512,512]{1,0:T(8,128)S(1)}, u32[]{:S(2)}) copy-start(f32[512,512]{1,0:T(8,128)S(1)} %fusion.3) | copy-start | bytes 3145732
  85.1 150.2 %reduce-scatter.2.cloned.1.call-start = ((), (), s32[]{:S(2)}) async-start(), calls=%async_computation.2 | async-start | bytes 2359296 | tf_op jit(solution)/shard_map/reduce_scatter | solution.py:22
  87.2 148.0 %copy-start.3 = (bf16[1024,512]{0,1:T(8,128)(2,1)S(1)}, bf16[1024,512]{0,1:T(8,128)(2,1)}, u32[]{:S(2)}) copy-start(bf16[1024,512]{0,1:T(8,128)(2,1)} %all-gather.2.cloned.1.call-done) | copy-start | bytes 3145732
  87.2 148.0 %copy-start.4 = (f32[1024,64]{0,1:T(8,128)S(1)}, f32[1024,64]{0,1:T(8,128)}, u32[]{:S(2)}) copy-start(f32[1024,64]{0,1:T(8,128)} %param.5) | copy-start | bytes 786436
Sparse Core Ops, SparseCore 0:
  10.7 42.8 all-gather.1
  61.1 20.0 all-reduce.5
  85.2 79.2 all-reduce.3
  167.9 67.2 reduce-scatter.1
where the time goes:
time: 245 us; the launch traced here: 244 us
  waiting for transfers between devices  212 us (87%)
  between operations  13.8 us (6%)
  matrix products  12.9 us (5%)
  other arithmetic  4.76 us (2%)
    psum x1, waiting for transfers between devices, shards(): gram = lax.psum(gram_local, 'frame')  77.3 us
    reduce_scatter x1, waiting for transfers between devices, shards(): lax.psum_scatter(jnp.einsum('kn,fn->kf', h_new, spectrogram, preferred_el...  70.7 us
    all_gather x1, waiting for transfers between devices, shards(): lax.all_gather(temps.astype(jnp.bfloat16), 'frame', axis=1, tiled=True)  43.7 us
    psum x1, waiting for transfers between devices, shards(): numer_h, denom_h = lax.psum((numer_h, denom_h), 'freq')  20.2 us
  transfers between devices with their start and end apart: 4, of which 4 were waited for; matrix products, arithmetic and copies ran while one was open for 1% of the time, Pallas kernels for 0%

commit v1 on v0

v1 whole, which is shorter than its diff:
```python
import jax
import jax.numpy as jnp
from jax import lax
from jax.experimental import pallas as pl
from jax.experimental.pallas import tpu as pltpu
from jax.sharding import PartitionSpec as P

BLOCK = 128
MESH = pl.DeviceIdType.MESH
NT = (((1,), (1,)), ((), ()))
F32 = jnp.float32
BF16 = jnp.bfloat16


def shards(spectrogram, templates, activations, score_mask):
    allowed = jnp.repeat(score_mask.astype(F32), BLOCK, axis=1)
    acts = activations * allowed
    temps = templates
    note_cols = temps.shape[1]
    h_bf = acts.astype(BF16)
    whole = lax.all_gather(temps.astype(BF16), "frame", axis=1, tiled=True)
    approx = jnp.dot(whole, h_bf, preferred_element_type=F32).astype(BF16)
    numer_h = jnp.einsum("fk,fn->kn", whole, spectrogram, preferred_element_type=F32)
    denom_h = jnp.einsum("fk,fn->kn", whole, approx, preferred_element_type=F32)
    numer_h, denom_h = lax.psum((numer_h, denom_h), "freq")
    acts = allowed * acts * numer_h / (denom_h + 1e-06)
    h_new = acts.astype(BF16)
    numer_w = lax.psum_scatter(
        jnp.einsum("kn,fn->kf", h_new, spectrogram, preferred_element_type=F32),
        "frame",
        scatter_dimension=0,
        tiled=True,
    ).T
    gram_local = jnp.einsum("kn,jn->kj", h_new, h_new, preferred_element_type=F32)
    gram = lax.psum(gram_local, "frame")
    own_cols = lax.dynamic_slice_in_dim(gram, lax.axis_index("frame") * note_cols, note_cols, 1)
    denom_w = jnp.dot(whole.astype(F32), own_cols, precision=lax.Precision.HIGHEST)
    temps = temps * numer_w / (denom_w + 1e-06)
    return (temps, acts)


def kernel(
    s_ref, t_ref, a_ref, m_ref, to_ref, ao_ref,
    wt, hbt, at, num, den, pnum, pden, hn, blk, xr, zr, gram,
    ws, wr, ns, nr, ds, dr, xs, xrs, zs, zrs, gs, gr,
):
    own, bins = t_ref.shape
    notes, frames = a_ref.shape
    half = notes // 2
    me = lax.axis_index("frame")
    c = lax.axis_index("freq")
    z, x = me // 2, me % 2
    across = z * 2 + 1 - x
    cp = 1 - c

    barrier = pltpu.get_barrier_semaphore()
    pl.semaphore_signal(barrier, inc=1, device_id={"frame": across}, device_id_type=MESH)
    pl.semaphore_signal(barrier, inc=1, device_id={"freq": cp}, device_id_type=MESH)

    @pl.when(z < 3)
    def _():
        pl.semaphore_signal(barrier, inc=1, device_id={"frame": me + 2}, device_id_type=MESH)

    @pl.when(z > 0)
    def _():
        pl.semaphore_signal(barrier, inc=1, device_id={"frame": me - 2}, device_id_type=MESH)

    wt[me] = t_ref[...].astype(BF16)
    pl.semaphore_wait(barrier, 2 + (z + 2) // 3 + (5 - z) // 3)

    def shard(idx, way):
        to = {0: across, 1: me + 2, 2: me - 2}[way]
        return pltpu.make_async_remote_copy(
            wt.at[idx], wt.at[idx], ws.at[way, idx], wr.at[idx],
            device_id={"frame": to}, device_id_type=MESH,
        )

    def numer_copy(idx):
        return pltpu.make_async_remote_copy(
            num.at[idx], pnum.at[idx], ns.at[idx], nr.at[idx],
            device_id={"freq": cp}, device_id_type=MESH,
        )

    def numer(idx):
        num[idx] = jnp.dot(wt[idx], s_ref[...], preferred_element_type=F32)
        numer_copy(idx).start()

    @pl.when(z < 3)
    def _():
        shard(me, 1).start()

    @pl.when(z > 0)
    def _():
        shard(me, 2).start()

    shard(me, 0).start()

    for b in range(frames // BLOCK):
        cols = slice(b * BLOCK, (b + 1) * BLOCK)
        held = a_ref[:, cols] * m_ref[:, b : b + 1].astype(F32)
        hbt[cols, :] = held.T.astype(BF16)
    numer(me)

    for s in range(1, 4):
        low, high = me - 2 * s, me + 2 * s

        @pl.when(z >= s)
        def _():
            shard(low, 0).wait_recv()

            @pl.when(z < 3)
            def _():
                shard(low, 1).start()

            shard(low, 0).start()

        @pl.when(z + s < 4)
        def _():
            shard(high, 0).wait_recv()

            @pl.when(z > 0)
            def _():
                shard(high, 2).start()

            shard(high, 0).start()

        @pl.when(z >= s)
        def _():
            numer(low)

        @pl.when(z + s < 4)
        def _():
            numer(high)

    def far(s):
        @pl.when(z >= s)
        def _():
            idx = across - 2 * s
            shard(idx, 0).wait_recv()
            numer(idx)

        if s:
            @pl.when(z + s < 4)
            def _():
                idx = across + 2 * s
                shard(idx, 0).wait_recv()
                numer(idx)

    for s in range(4):
        far(s)

    step = 256

    @pl.loop(0, bins // step)
    def _(j):
        cols = pl.ds(pl.multiple_of(j * step, step), step)
        w = wt[:, :, cols].reshape(notes, step)
        at[:, cols] = jnp.dot(hbt[...], w, preferred_element_type=F32).astype(BF16)

    def denom_copy(j):
        return pltpu.make_async_remote_copy(
            den.at[j], pden.at[j], ds.at[j], dr.at[j],
            device_id={"freq": cp}, device_id_type=MESH,
        )

    for j in range(2):
        w = wt[j * 4 : j * 4 + 4].reshape(half, bins)
        den[j] = lax.dot_general(w, at[...], NT, preferred_element_type=F32)
        denom_copy(j).start()

    for i in range(8):
        numer_copy(i).wait_recv()

    for j in range(2):
        denom_copy(j).wait_recv()
        rows = slice(j * half, (j + 1) * half)
        for b in range(frames // BLOCK):
            cols = slice(b * BLOCK, (b + 1) * BLOCK)
            allowed = m_ref[rows, b : b + 1].astype(F32)
            up = (num[j * 4 : j * 4 + 4, :, cols] + pnum[j * 4 : j * 4 + 4, :, cols]).reshape(half, BLOCK)
            under = den[j, :, cols] + pden[j, :, cols]
            new = allowed * (a_ref[rows, cols] * allowed) * up / (under + 1e-06)
            ao_ref[rows, cols] = new
            hn[rows, cols] = new.astype(BF16)

    order = [3 * (1 - z // 2), 0, 1 + z % 2, z]
    order[1] = 6 - order[0] - order[2] - z
    mine = pl.ds(pl.multiple_of(c * half, half), half)

    def partial(idx):
        h = hn[pl.ds(pl.multiple_of(idx * own, own), own), :]
        blk[idx, :, :bins] = lax.dot_general(h, s_ref[...], NT, preferred_element_type=F32)
        blk[idx, :, bins:] = lax.dot_general(h, hn[mine, :], NT, preferred_element_type=F32)

    def x_copy(d):
        return pltpu.make_async_remote_copy(
            blk.at[2 * d + 1 - x], xr.at[d], xs.at[d], xrs.at[d],
            device_id={"frame": across}, device_id_type=MESH,
        )

    def z_copy(d, way):
        to = me + 2 if way else me - 2
        return pltpu.make_async_remote_copy(
            blk.at[2 * d + x], zr.at[way, d], zs.at[d], zrs.at[way, d],
            device_id={"frame": to}, device_id_type=MESH,
        )

    for d in order:
        partial(2 * d + 1 - x)
        x_copy(d).start()

    for d in order[:3]:
        idx = 2 * d + x
        partial(idx)
        x_copy(d).wait_recv()
        blk[idx] += xr[d]

        @pl.when(d > z)
        def _():
            @pl.when(z > 0)
            def _():
                z_copy(d, 1).wait_recv()
                blk[idx] += zr[1, d]

            z_copy(d, 1).start()

        @pl.when(d < z)
        def _():
            @pl.when(z < 3)
            def _():
                z_copy(d, 0).wait_recv()
                blk[idx] += zr[0, d]

            z_copy(d, 0).start()

    partial(me)
    x_copy(z).wait_recv()
    blk[me] += xr[z]

    @pl.when(z > 0)
    def _():
        z_copy(z, 1).wait_recv()
        blk[me] += zr[1, z]

    @pl.when(z < 3)
    def _():
        z_copy(z, 0).wait_recv()
        blk[me] += zr[0, z]

    gram[c] = blk[me, :, bins:]
    share = pltpu.make_async_remote_copy(
        gram.at[c], gram.at[c], gs, gr, device_id={"freq": cp}, device_id_type=MESH
    )
    share.start()
    share.wait_recv()

    total = jnp.zeros((own, bins), F32)
    for j in range(2):
        g = gram[j]
        hi = g.astype(BF16)
        lo = (g - hi.astype(F32)).astype(BF16)
        w = wt[j * 4 : j * 4 + 4].reshape(half, bins)
        both = jnp.dot(jnp.concatenate([hi, lo], 0), w, preferred_element_type=F32)
        total = total + both[:own] + both[own:]
    to_ref[...] = t_ref[...] * blk[me, :, :bins] / (total + 1e-06)

    share.wait_send()
    for j in range(2):
        denom_copy(j).wait_send()
    for i in range(8):
        numer_copy(i).wait_send()
    for d in range(4):
        x_copy(d).wait_send()
        shard(2 * d + x, 0).wait_send()

        @pl.when(d != z)
        def _():
            z_copy(d, 0).wait_send()

        @pl.when(jnp.logical_and(d <= z, z < 3))
        def _():
            shard(2 * d + x, 1).wait_send()

        @pl.when(jnp.logical_and(d >= z, z > 0))
        def _():
            shard(2 * d + x, 2).wait_send()


def fused(spectrogram, templates, activations, score_mask):
    bins, own = templates.shape
    notes, frames = activations.shape
    half = notes // 2
    dma = pltpu.SemaphoreType.DMA
    wide = bins + half
    turned, acts = pl.pallas_call(
        kernel,
        out_shape=(
            jax.ShapeDtypeStruct((own, bins), F32),
            jax.ShapeDtypeStruct((notes, frames), F32),
        ),
        in_specs=[pl.BlockSpec(memory_space=pltpu.VMEM)] * 4,
        out_specs=[pl.BlockSpec(memory_space=pltpu.VMEM)] * 2,
        scratch_shapes=[
            pltpu.VMEM((8, own, bins), BF16),
            pltpu.VMEM((frames, notes), BF16),
            pltpu.VMEM((frames, bins), BF16),
            pltpu.VMEM((8, own, frames), F32),
            pltpu.VMEM((2, half, frames), F32),
            pltpu.VMEM((8, own, frames), F32),
            pltpu.VMEM((2, half, frames), F32),
            pltpu.VMEM((notes, frames), BF16),
            pltpu.VMEM((8, own, wide), F32),
            pltpu.VMEM((4, own, wide), F32),
            pltpu.VMEM((2, 4, own, wide), F32),
            pltpu.VMEM((2, own, half), F32),
            dma((3, 8)), dma((8,)), dma((8,)), dma((8,)), dma((2,)), dma((2,)),
            dma((4,)), dma((4,)), dma((4,)), dma((2, 4)), dma(()), dma(()),
        ],
        compiler_params=pltpu.CompilerParams(
            collective_id=0, has_side_effects=True, vmem_limit_bytes=48 * 1024 * 1024
        ),
    )(spectrogram, templates.T, activations, score_mask)
    return turned.T, acts


def solution(mesh):
    return jax.shard_map(
        fused if mesh.shape["frame"] == 8 else shards,
        mesh=mesh,
        in_specs=(
            P("freq", ("parts", "frame")),
            P(("parts", "freq"), "frame"),
            P(None, ("parts", "frame")),
            P(None, ("parts", "frame")),
        ),
        out_specs=(P(("parts", "freq"), "frame"), P(None, ("parts", "frame"))),
        check_vma=False,
    )
```

time: 245 us -> 65 us (0.27)
  waiting for transfers between devices: 212 us -> 0 us
  Pallas kernels: 0 us -> 58.7 us
  between operations: 13.8 us -> 0.66 us
  matrix products: 12.9 us -> 0 us
  other arithmetic: 4.76 us -> 0 us
  local copies, waits for them, and re-layouts: 0.77 us -> 5.07 us
    psum x2 -> x0, waiting for transfers between devices: 97.4 us -> none  [the longest x1 77.3 us: shards(): gram = lax.psum(gram_local, 'frame')]
    reduce_scatter x1 -> x0, waiting for transfers between devices: 70.7 us -> none  [shards(): lax.psum_scatter(jnp.einsum('kn,fn->kf', h_new, spectrogram, preferred_el...]
    pallas_call x0 -> x1, Pallas kernels: none -> 58.7 us  [fused(): pl.pallas_call(kernel, out_shape=(jax.ShapeDtypeStruct((own, bins), F32),...]
    all_gather x1 -> x0, waiting for transfers between devices: 43.7 us -> none  [shards(): lax.all_gather(temps.astype(jnp.bfloat16), 'frame', axis=1, tiled=True)]
    dot_general x5 -> x0, matrix products: 12.9 us -> none  [the longest x1 3.88 us: shards(): jnp.einsum('fk,fn->kn', whole, approx, preferred_element_type=jnp.float32)]
    unnamed x10 -> x9, local copies, waits for them, and re-layouts: 0.03 us -> 5.07 us
  transfers between devices with their start and end apart: 4 -> 0, of which waited for: 4 -> 0; matrix products, arithmetic and copies ran while one was open for 1% -> 0% of each run, Pallas kernels for 0% -> 0%
where the time goes in v1:
time: 65 us; the launch traced here: 64.4 us
  Pallas kernels  58.7 us (90%)
  local copies, waits for them, and re-layouts  5.07 us (8%)
  between operations  0.66 us (1%)
    pallas_call x1, Pallas kernels, fused(): pl.pallas_call(kernel, out_shape=(jax.ShapeDtypeStruct((own, bins), F32),...  58.7 us
    unnamed x9, local copies, waits for them, and re-layouts  5.07 us

profile of v1, /device:TPU:0, one launch (start us, length us, event | category | flops | bytes accessed | tf_op | source)
XLA Modules:
  0.0 64.4 jit_solution(10902263073300510780)
XLA Ops:
  0.6 0.0 copy-start.2
  0.6 0.9 %copy.6.m_ref = s32[512,4]{1,0:T(8,128)S(1)} copy(s32[512,4]{0,1:T(4,128)} %param.7) | data formatting | bytes 16384 | tf_op args[3]
  1.5 0.1 copy-done.2
  1.6 0.0 copy-start
  1.6 1.2 %copy-done = bf16[1024,512]{1,0:T(8,128)(2,1)S(1)} copy-done((bf16[1024,512]{1,0:T(8,128)(2,1)S(1)}, bf16[1024,512]{1,0:T(8,128)(2,1)}, u32[]{:S(2)}) %copy-start) | copy-done | bytes 1048600
  2.8 0.0 copy-start.1
  2.8 1.2 %copy-done.1 = f32[512,512]{1,0:T(8,128)S(1)} copy-done((f32[512,512]{1,0:T(8,128)S(1)}, f32[512,512]{1,0:T(8,128)}, u32[]{:S(2)}) %copy-start.1) | copy-done | bytes 1048600
  4.0 58.7 %shard_map.59 = (f32[64,1024]{1,0:T(8,128)S(1)}, f32[512,512]{1,0:T(8,128)S(1)}) custom-call(bf16[1024,512]{1,0:T(8,128)(2,1)S(1)} %copy-done, f32[64,1024]{1,0:T(8,128)S(1)} %bitcast.2, f32[512,512]{1,0:T(8,128)S(1)} %copy-done.1, s32[512,4]{1,0:T(8,128)S(1)} %copy.6.m_ref), custom_call_target="tpu_custom_call" | custom-call | tf_op jit(solution)/shard_map/pallas_call | solution.py:295
  62.7 0.7 %copy.9 = f32[1024,64]{0,1:T(8,128)} copy(f32[1024,64]{0,1:T(8,128)S(1)} %bitcast.3) | data formatting | bytes 524288
  63.4 1.0 %copy.10 = f32[512,512]{1,0:T(8,128)} copy(f32[512,512]{1,0:T(8,128)S(1)} %get-tuple-element.9) | data formatting | bytes 2097152
Async XLA Ops:
  0.6 1.0 %copy-start.2 = (f32[1024,64]{0,1:T(8,128)S(1)}, f32[1024,64]{0,1:T(8,128)}, u32[]{:S(2)}) copy-start(f32[1024,64]{0,1:T(8,128)} %param.5) | copy-start | bytes 786436
  1.6 1.2 %copy-start = (bf16[1024,512]{1,0:T(8,128)(2,1)S(1)}, bf16[1024,512]{1,0:T(8,128)(2,1)}, u32[]{:S(2)}) copy-start(bf16[1024,512]{1,0:T(8,128)(2,1)} %s_ref.1) | copy-start | bytes 3145732
  2.8 1.2 %copy-start.1 = (f32[512,512]{1,0:T(8,128)S(1)}, f32[512,512]{1,0:T(8,128)}, u32[]{:S(2)}) copy-start(f32[512,512]{1,0:T(8,128)} %a_ref.1) | copy-start | bytes 3145732

commit v2 on v1

--- a/solution.py
+++ b/solution.py
@@ -40,12 +40,13 @@
 
 
 def kernel(
-    s_ref, t_ref, a_ref, m_ref, to_ref, ao_ref,
-    wt, hbt, at, num, den, pnum, pden, hn, blk, xr, zr, gram,
-    ws, wr, ns, nr, ds, dr, xs, xrs, zs, zrs, gs, gr,
+    s_hbm, t_ref, a_hbm, m_ref, to_ref, ao_ref,
+    s_ref, a_ref, mt, wt, hbt, at, num, den, pnum, pden, hn, blk, out, xr, zr, gram,
+    ls, ws, wr, ns, nr, ds, dr, xs, xrs, zs, zrs, gs, gr,
 ):
     own, bins = t_ref.shape
     notes, frames = a_ref.shape
+    wide = bins + notes // 2
     half = notes // 2
     me = lax.axis_index("frame")
     c = lax.axis_index("freq")
@@ -53,6 +54,11 @@
     across = z * 2 + 1 - x
     cp = 1 - c
 
+    load_a = pltpu.make_async_copy(a_hbm, a_ref, ls.at[0])
+    load_s = pltpu.make_async_copy(s_hbm, s_ref, ls.at[1])
+    load_a.start()
+    load_s.start()
+
     barrier = pltpu.get_barrier_semaphore()
     pl.semaphore_signal(barrier, inc=1, device_id={"frame": across}, device_id_type=MESH)
     pl.semaphore_signal(barrier, inc=1, device_id={"freq": cp}, device_id_type=MESH)
@@ -95,10 +101,14 @@
 
     shard(me, 0).start()
 
+    flags = m_ref[...].astype(F32)
+    mt[...] = jnp.concatenate([flags, flags], 0).T
+    load_a.wait()
     for b in range(frames // BLOCK):
         cols = slice(b * BLOCK, (b + 1) * BLOCK)
-        held = a_ref[:, cols] * m_ref[:, b : b + 1].astype(F32)
+        held = a_ref[:, cols] * mt[:, b : b + 1]
         hbt[cols, :] = held.T.astype(BF16)
+    load_s.wait()
     numer(me)
 
     for s in range(1, 4):
@@ -176,7 +186,7 @@
         rows = slice(j * half, (j + 1) * half)
         for b in range(frames // BLOCK):
             cols = slice(b * BLOCK, (b + 1) * BLOCK)
-            allowed = m_ref[rows, b : b + 1].astype(F32)
+            allowed = mt[rows, b : b + 1]
             up = (num[j * 4 : j * 4 + 4, :, cols] + pnum[j * 4 : j * 4 + 4, :, cols]).reshape(half, BLOCK)
             under = den[j, :, cols] + pden[j, :, cols]
             new = allowed * (a_ref[rows, cols] * allowed) * up / (under + 1e-06)
@@ -192,36 +202,57 @@
         blk[idx, :, :bins] = lax.dot_general(h, s_ref[...], NT, preferred_element_type=F32)
         blk[idx, :, bins:] = lax.dot_general(h, hn[mine, :], NT, preferred_element_type=F32)
 
+    def encode(idx):
+        powers = []
+        for cols in (slice(0, bins), slice(bins, wide)):
+            v = blk[idx, :, cols]
+            top = jnp.max(v, axis=1, keepdims=True)
+            power = jnp.ceil(jnp.log2(jnp.maximum(top, 1e-30)))
+            q = jnp.minimum(jnp.round(v * jnp.exp2(16.0 - power)) - 32768.0, 32767.0)
+            out[idx, :, cols] = q.astype(jnp.int32).astype(jnp.int16)
+            powers.append(jnp.broadcast_to(power, (own, BLOCK)))
+        lane = lax.broadcasted_iota(jnp.int32, (own, BLOCK), 1)
+        power = jnp.where(lane < BLOCK // 2, powers[0], powers[1])
+        out[idx, :, wide:] = power.astype(jnp.int32).astype(jnp.int16)
+
+    def add(idx, ref):
+        scale = jnp.exp2(ref[:, wide:].astype(jnp.int32).astype(F32) - 16.0)
+        for cols, col in ((slice(0, bins), 0), (slice(bins, wide), BLOCK - 1)):
+            v = ref[:, cols].astype(jnp.int32).astype(F32) + 32768.0
+            blk[idx, :, cols] += v * scale[:, col : col + 1]
+
     def x_copy(d):
         return pltpu.make_async_remote_copy(
-            blk.at[2 * d + 1 - x], xr.at[d], xs.at[d], xrs.at[d],
+            out.at[2 * d + 1 - x], xr.at[d], xs.at[d], xrs.at[d],
             device_id={"frame": across}, device_id_type=MESH,
         )
 
     def z_copy(d, way):
         to = me + 2 if way else me - 2
         return pltpu.make_async_remote_copy(
-            blk.at[2 * d + x], zr.at[way, d], zs.at[d], zrs.at[way, d],
+            out.at[2 * d + x], zr.at[way, d], zs.at[d], zrs.at[way, d],
             device_id={"frame": to}, device_id_type=MESH,
         )
 
     for d in order:
         partial(2 * d + 1 - x)
+        encode(2 * d + 1 - x)
         x_copy(d).start()
 
     for d in order[:3]:
         idx = 2 * d + x
         partial(idx)
         x_copy(d).wait_recv()
-        blk[idx] += xr[d]
+        add(idx, xr.at[d])
 
         @pl.when(d > z)
         def _():
             @pl.when(z > 0)
             def _():
                 z_copy(d, 1).wait_recv()
-                blk[idx] += zr[1, d]
-
+                add(idx, zr.at[1, d])
+
+            encode(idx)
             z_copy(d, 1).start()
 
         @pl.when(d < z)
@@ -229,23 +260,24 @@
             @pl.when(z < 3)
             def _():
                 z_copy(d, 0).wait_recv()
-                blk[idx] += zr[0, d]
-
+                add(idx, zr.at[0, d])
+
+            encode(idx)
             z_copy(d, 0).start()
 
     partial(me)
     x_copy(z).wait_recv()
-    blk[me] += xr[z]
+    add(me, xr.at[z])
 
     @pl.when(z > 0)
     def _():
         z_copy(z, 1).wait_recv()
-        blk[me] += zr[1, z]
+        add(me, zr.at[1, z])
 
     @pl.when(z < 3)
     def _():
         z_copy(z, 0).wait_recv()
-        blk[me] += zr[0, z]
+        add(me, zr.at[0, z])
 
     gram[c] = blk[me, :, bins:]
     share = pltpu.make_async_remote_copy(
@@ -298,9 +330,12 @@
             jax.ShapeDtypeStruct((own, bins), F32),
             jax.ShapeDtypeStruct((notes, frames), F32),
         ),
-        in_specs=[pl.BlockSpec(memory_space=pltpu.VMEM)] * 4,
+        in_specs=[pl.BlockSpec(memory_space=m) for m in (pltpu.HBM, pltpu.VMEM, pltpu.HBM, pltpu.VMEM)],
         out_specs=[pl.BlockSpec(memory_space=pltpu.VMEM)] * 2,
         scratch_shapes=[
+            pltpu.VMEM((bins, frames), BF16),
+            pltpu.VMEM((notes, frames), F32),
+            pltpu.VMEM((notes, 8), F32),
             pltpu.VMEM((8, own, bins), BF16),
             pltpu.VMEM((frames, notes), BF16),
             pltpu.VMEM((frames, bins), BF16),
@@ -310,16 +345,17 @@
             pltpu.VMEM((2, half, frames), F32),
             pltpu.VMEM((notes, frames), BF16),
             pltpu.VMEM((8, own, wide), F32),
-            pltpu.VMEM((4, own, wide), F32),
-            pltpu.VMEM((2, 4, own, wide), F32),
+            pltpu.VMEM((8, own, wide + BLOCK), jnp.int16),
+            pltpu.VMEM((4, own, wide + BLOCK), jnp.int16),
+            pltpu.VMEM((2, 4, own, wide + BLOCK), jnp.int16),
             pltpu.VMEM((2, own, half), F32),
-            dma((3, 8)), dma((8,)), dma((8,)), dma((8,)), dma((2,)), dma((2,)),
+            dma((2,)), dma((3, 8)), dma((8,)), dma((8,)), dma((8,)), dma((2,)), dma((2,)),
             dma((4,)), dma((4,)), dma((4,)), dma((2, 4)), dma(()), dma(()),
         ],
         compiler_params=pltpu.CompilerParams(
             collective_id=0, has_side_effects=True, vmem_limit_bytes=48 * 1024 * 1024
         ),
-    )(spectrogram, templates.T, activations, score_mask)
+    )(spectrogram, templates.T, activations, score_mask.T)
     return turned.T, acts
 
 

time: 65 us -> 54.8 us (0.84)
  the two profiles are of different devices: /device:TPU:0 before, /device:TPU:9 now
where the time goes in v2:
time: 54.8 us; the launch traced here: 54.5 us
  Pallas kernels  48.1 us (88%)
  local copies, waits for them, and re-layouts  5.76 us (11%)
  between operations  0.65 us (1%)
    pallas_call x1, Pallas kernels, fused(): pl.pallas_call(kernel, out_shape=(jax.ShapeDtypeStruct((own, bins), F32),...  48.1 us
    unnamed x10, local copies, waits for them, and re-layouts  5.76 us

profile of v2, /device:TPU:9, one launch (start us, length us, event | category | flops | bytes accessed | tf_op | source)
XLA Modules:
  0.0 54.5 jit_solution(12702171636321180432)
XLA Ops:
  0.6 0.0 copy-start
  0.6 1.2 %copy-done = bf16[1024,512]{1,0:T(8,128)(2,1)S(1)} copy-done((bf16[1024,512]{1,0:T(8,128)(2,1)S(1)}, bf16[1024,512]{1,0:T(8,128)(2,1)}, u32[]{:S(2)}) %copy-start) | copy-done | bytes 1048600
  1.9 0.0 copy-start.1
  1.9 1.2 %copy-done.1 = f32[512,512]{1,0:T(8,128)S(1)} copy-done((f32[512,512]{1,0:T(8,128)S(1)}, f32[512,512]{1,0:T(8,128)}, u32[]{:S(2)}) %copy-start.1) | copy-done | bytes 1048600
  3.1 0.0 copy-start.2
  3.1 0.9 %copy-done.2 = f32[1024,64]{0,1:T(8,128)S(1)} copy-done((f32[1024,64]{0,1:T(8,128)S(1)}, f32[1024,64]{0,1:T(8,128)}, u32[]{:S(2)}) %copy-start.2) | copy-done | bytes 262168
  4.0 0.0 copy-start.3
  4.0 0.7 %copy-done.3 = s32[512,4]{0,1:T(4,128)S(1)} copy-done((s32[512,4]{0,1:T(4,128)S(1)}, s32[512,4]{0,1:T(4,128)}, u32[]{:S(2)}) %copy-start.3) | copy-done | bytes 8216
  4.7 48.1 %shard_map.59 = (f32[64,1024]{1,0:T(8,128)S(1)}, f32[512,512]{1,0:T(8,128)S(1)}) custom-call(bf16[1024,512]{1,0:T(8,128)(2,1)S(1)} %copy-done, f32[64,1024]{1,0:T(8,128)S(1)} %bitcast.3, f32[512,512]{1,0:T(8,128)S(1)} %copy-done.1, s32[4,512]{1,0:T(4,128)S(1)} %bitcast.5), custom_call_target="tpu_custom_call" | custom-call | tf_op jit(solution)/shard_map/pallas_call | solution.py:327
  52.9 0.7 %copy.8 = f32[1024,64]{0,1:T(8,128)} copy(f32[1024,64]{0,1:T(8,128)S(1)} %bitcast.4) | data formatting | bytes 524288
  53.6 1.0 %copy.9 = f32[512,512]{1,0:T(8,128)} copy(f32[512,512]{1,0:T(8,128)S(1)} %get-tuple-element.9) | data formatting | bytes 2097152
Async XLA Ops:
  0.6 1.2 %copy-start = (bf16[1024,512]{1,0:T(8,128)(2,1)S(1)}, bf16[1024,512]{1,0:T(8,128)(2,1)}, u32[]{:S(2)}) copy-start(bf16[1024,512]{1,0:T(8,128)(2,1)} %s_hbm.1) | copy-start | bytes 3145732
  1.9 1.2 %copy-start.1 = (f32[512,512]{1,0:T(8,128)S(1)}, f32[512,512]{1,0:T(8,128)}, u32[]{:S(2)}) copy-start(f32[512,512]{1,0:T(8,128)} %a_hbm.1) | copy-start | bytes 3145732
  3.1 0.9 %copy-start.2 = (f32[1024,64]{0,1:T(8,128)S(1)}, f32[1024,64]{0,1:T(8,128)}, u32[]{:S(2)}) copy-start(f32[1024,64]{0,1:T(8,128)} %param.5) | copy-start | bytes 786436
  4.0 0.7 %copy-start.3 = (s32[512,4]{0,1:T(4,128)S(1)}, s32[512,4]{0,1:T(4,128)}, u32[]{:S(2)}) copy-start(s32[512,4]{0,1:T(4,128)} %param.7) | copy-start | bytes 24580

commit v3 on v2

--- a/solution.py
+++ b/solution.py
@@ -40,8 +40,8 @@
 
 
 def kernel(
-    s_hbm, t_ref, a_hbm, m_ref, to_ref, ao_ref,
-    s_ref, a_ref, mt, wt, hbt, at, num, den, pnum, pden, hn, blk, out, xr, zr, gram,
+    s_hbm, t_hbm, a_hbm, m_hbm, to_ref, ao_hbm,
+    s_ref, t_ref, a_ref, m_ref, ao_ref, mt, wt, hbt, at, num, den, pnum, pden, hn, blk, out, xr, zr, gram,
     ls, ws, wr, ns, nr, ds, dr, xs, xrs, zs, zrs, gs, gr,
 ):
     own, bins = t_ref.shape
@@ -56,8 +56,10 @@
 
     load_a = pltpu.make_async_copy(a_hbm, a_ref, ls.at[0])
     load_s = pltpu.make_async_copy(s_hbm, s_ref, ls.at[1])
-    load_a.start()
-    load_s.start()
+    load_t = pltpu.make_async_copy(t_hbm, t_ref, ls.at[2])
+    load_m = pltpu.make_async_copy(m_hbm, m_ref, ls.at[3])
+    for load in (load_t, load_m, load_a, load_s):
+        load.start()
 
     barrier = pltpu.get_barrier_semaphore()
     pl.semaphore_signal(barrier, inc=1, device_id={"frame": across}, device_id_type=MESH)
@@ -71,15 +73,27 @@
     def _():
         pl.semaphore_signal(barrier, inc=1, device_id={"frame": me - 2}, device_id_type=MESH)
 
+    load_t.wait()
     wt[me] = t_ref[...].astype(BF16)
     pl.semaphore_wait(barrier, 2 + (z + 2) // 3 + (5 - z) // 3)
 
-    def shard(idx, way):
+    def shard(idx, way, part):
         to = {0: across, 1: me + 2, 2: me - 2}[way]
+        rows = pl.ds(part * (own // 2), own // 2)
         return pltpu.make_async_remote_copy(
-            wt.at[idx], wt.at[idx], ws.at[way, idx], wr.at[idx],
+            wt.at[idx, rows], wt.at[idx, rows], ws.at[way, idx, part], wr.at[idx, part],
             device_id={"frame": to}, device_id_type=MESH,
         )
+
+    def send(idx, way):
+        for part in range(2):
+            shard(idx, way, part).start()
+
+    def arrive(idx):
+        for part in range(2):
+            shard(idx, 0, part).wait_recv()
+
+    first, last = 1 - x, 7 - x
 
     def numer_copy(idx):
         return pltpu.make_async_remote_copy(
@@ -93,14 +107,15 @@
 
     @pl.when(z < 3)
     def _():
-        shard(me, 1).start()
+        send(me, 1)
 
     @pl.when(z > 0)
     def _():
-        shard(me, 2).start()
-
-    shard(me, 0).start()
-
+        send(me, 2)
+
+    send(me, 0)
+
+    load_m.wait()
     flags = m_ref[...].astype(F32)
     mt[...] = jnp.concatenate([flags, flags], 0).T
     load_a.wait()
@@ -109,55 +124,108 @@
         held = a_ref[:, cols] * mt[:, b : b + 1]
         hbt[cols, :] = held.T.astype(BF16)
     load_s.wait()
-    numer(me)
-
-    for s in range(1, 4):
+
+    def forward(s):
         low, high = me - 2 * s, me + 2 * s
 
         @pl.when(z >= s)
         def _():
-            shard(low, 0).wait_recv()
+            arrive(low)
 
             @pl.when(z < 3)
             def _():
-                shard(low, 1).start()
-
-            shard(low, 0).start()
+                send(low, 1)
+
+            shard(low, 0, 0).start()
+
+            @pl.when(z > s)
+            def _():
+                shard(low, 0, 1).start()
 
         @pl.when(z + s < 4)
         def _():
-            shard(high, 0).wait_recv()
+            arrive(high)
 
             @pl.when(z > 0)
             def _():
-                shard(high, 2).start()
-
-            shard(high, 0).start()
-
+                send(high, 2)
+
+            shard(high, 0, 0).start()
+
+            @pl.when(z + s < 3)
+            def _():
+                shard(high, 0, 1).start()
+
+    def near(s):
         @pl.when(z >= s)
         def _():
-            numer(low)
+            numer(me - 2 * s)
 
         @pl.when(z + s < 4)
         def _():
-            numer(high)
+            numer(me + 2 * s)
 
     def far(s):
         @pl.when(z >= s)
         def _():
             idx = across - 2 * s
-            shard(idx, 0).wait_recv()
+            shard(idx, 0, 0).wait_recv()
+
+            @pl.when(jnp.logical_or(z > s, z == 3))
+            def _():
+                shard(idx, 0, 1).wait_recv()
+
             numer(idx)
 
-        if s:
-            @pl.when(z + s < 4)
-            def _():
-                idx = across + 2 * s
-                shard(idx, 0).wait_recv()
-                numer(idx)
-
-    for s in range(4):
-        far(s)
+        @pl.when(z + s < 4)
+        def _():
+            idx = across + 2 * s
+            shard(idx, 0, 0).wait_recv()
+
+            @pl.when(jnp.logical_or(z + s < 3, z == 0))
+            def _():
+                shard(idx, 0, 1).wait_recv()
+
+            numer(idx)
+
+    def along(up, down):
+        @pl.when(z == up)
+        def _():
+            shard(first, 0, 1).wait_recv()
+            shard(first, 1, 1).start()
+
+        @pl.when(z == down)
+        def _():
+            shard(last, 0, 1).wait_recv()
+            shard(last, 2, 1).start()
+
+    forward(1)
+    arrive(across)
+
+    @pl.when(z == 0)
+    def _():
+        shard(first, 1, 1).start()
+
+    @pl.when(z == 3)
+    def _():
+        shard(last, 2, 1).start()
+
+    numer(me)
+    numer(across)
+    forward(2)
+    near(1)
+    along(1, 2)
+    far(1)
+    forward(3)
+    near(2)
+    along(2, 1)
+    near(3)
+    far(2)
+    far(3)
+
+    def store(j):
+        rows = pl.ds(j * half, half)
+        return pltpu.make_async_copy(ao_ref.at[rows], ao_hbm.at[rows], ls.at[4 + j])
 
     step = 256
 
@@ -192,6 +260,7 @@
             new = allowed * (a_ref[rows, cols] * allowed) * up / (under + 1e-06)
             ao_ref[rows, cols] = new
             hn[rows, cols] = new.astype(BF16)
+        store(j).start()
 
     order = [3 * (1 - z // 2), 0, 1 + z % 2, z]
     order[1] = 6 - order[0] - order[2] - z
@@ -299,11 +368,16 @@
     share.wait_send()
     for j in range(2):
         denom_copy(j).wait_send()
+        store(j).wait()
     for i in range(8):
         numer_copy(i).wait_send()
     for d in range(4):
         x_copy(d).wait_send()
-        shard(2 * d + x, 0).wait_send()
+        shard(2 * d + x, 0, 0).wait_send()
+
+        @pl.when(d == z if d in (0, 3) else d >= 0 * z)
+        def _():
+            shard(2 * d + x, 0, 1).wait_send()
 
         @pl.when(d != z)
         def _():
@@ -311,11 +385,21 @@
 
         @pl.when(jnp.logical_and(d <= z, z < 3))
         def _():
-            shard(2 * d + x, 1).wait_send()
+            for part in range(2):
+                shard(2 * d + x, 1, part).wait_send()
 
         @pl.when(jnp.logical_and(d >= z, z > 0))
         def _():
-            shard(2 * d + x, 2).wait_send()
+            for part in range(2):
+                shard(2 * d + x, 2, part).wait_send()
+
+    @pl.when(z < 3)
+    def _():
+        shard(first, 1, 1).wait_send()
+
+    @pl.when(z > 0)
+    def _():
+        shard(last, 2, 1).wait_send()
 
 
 def fused(spectrogram, templates, activations, score_mask):
@@ -330,10 +414,13 @@
             jax.ShapeDtypeStruct((own, bins), F32),
             jax.ShapeDtypeStruct((notes, frames), F32),
         ),
-        in_specs=[pl.BlockSpec(memory_space=m) for m in (pltpu.HBM, pltpu.VMEM, pltpu.HBM, pltpu.VMEM)],
-        out_specs=[pl.BlockSpec(memory_space=pltpu.VMEM)] * 2,
+        in_specs=[pl.BlockSpec(memory_space=pltpu.HBM)] * 4,
+        out_specs=[pl.BlockSpec(memory_space=m) for m in (pltpu.VMEM, pltpu.HBM)],
         scratch_shapes=[
             pltpu.VMEM((bins, frames), BF16),
+            pltpu.VMEM((own, bins), F32),
+            pltpu.VMEM((notes, frames), F32),
+            pltpu.VMEM((frames // BLOCK, notes), jnp.int32),
             pltpu.VMEM((notes, frames), F32),
             pltpu.VMEM((notes, 8), F32),
             pltpu.VMEM((8, own, bins), BF16),
@@ -349,11 +436,11 @@
             pltpu.VMEM((4, own, wide + BLOCK), jnp.int16),
             pltpu.VMEM((2, 4, own, wide + BLOCK), jnp.int16),
             pltpu.VMEM((2, own, half), F32),
-            dma((2,)), dma((3, 8)), dma((8,)), dma((8,)), dma((8,)), dma((2,)), dma((2,)),
+            dma((6,)), dma((3, 8, 2)), dma((8, 2)), dma((8,)), dma((8,)), dma((2,)), dma((2,)),
             dma((4,)), dma((4,)), dma((4,)), dma((2, 4)), dma(()), dma(()),
         ],
         compiler_params=pltpu.CompilerParams(
-            collective_id=0, has_side_effects=True, vmem_limit_bytes=48 * 1024 * 1024
+            collective_id=0, has_side_effects=True, vmem_limit_bytes=60 * 1024 * 1024
         ),
     )(spectrogram, templates.T, activations, score_mask.T)
     return turned.T, acts

time: 54.8 us -> 54.2 us (0.989)
  the two profiles are of different devices: /device:TPU:9 before, /device:TPU:0 now
where the time goes in v3:
time: 54.2 us; the launch traced here: 54 us
  Pallas kernels  49.4 us (91%)
  local copies, waits for them, and re-layouts  3.93 us (7%)
  between operations  0.64 us (1%)
    pallas_call x1, Pallas kernels, fused(): pl.pallas_call(kernel, out_shape=(jax.ShapeDtypeStruct((own, bins), F32),...  49.4 us
    unnamed x2, local copies, waits for them, and re-layouts  3.93 us

profile of v3, /device:TPU:0, one launch (start us, length us, event | category | flops | bytes accessed | tf_op | source)
XLA Modules:
  0.0 54.0 jit_solution(7494512775195381456)
XLA Ops:
  0.6 49.4 %shard_map.59 = (f32[64,1024]{1,0:T(8,128)}, f32[512,512]{1,0:T(8,128)}) custom-call(bf16[1024,512]{1,0:T(8,128)(2,1)} %s_hbm.1, f32[64,1024]{1,0:T(8,128)} %bitcast.3, f32[512,512]{1,0:T(8,128)} %a_hbm.1, s32[4,512]{1,0:T(4,128)} %bitcast.5), custom_call_target="tpu_custom_call" | custom-call | tf_op jit(solution)/shard_map/pallas_call | solution.py:411
  50.1 1.7 %copy.8 = f32[1024,64]{0,1:T(8,128)} copy(f32[1024,64]{0,1:T(8,128)} %bitcast.4) | data formatting | bytes 524288
  51.7 2.3 %copy.9 = f32[512,512]{1,0:T(8,128)} copy(f32[512,512]{1,0:T(8,128)} %get-tuple-element.9) | data formatting | bytes 2097152

commit v4 on v3

--- a/solution.py
+++ b/solution.py
@@ -105,6 +105,8 @@
         num[idx] = jnp.dot(wt[idx], s_ref[...], preferred_element_type=F32)
         numer_copy(idx).start()
 
+    send(me, 0)
+
     @pl.when(z < 3)
     def _():
         send(me, 1)
@@ -112,8 +114,6 @@
     @pl.when(z > 0)
     def _():
         send(me, 2)
-
-    send(me, 0)
 
     load_m.wait()
     flags = m_ref[...].astype(F32)
@@ -284,9 +284,10 @@
         power = jnp.where(lane < BLOCK // 2, powers[0], powers[1])
         out[idx, :, wide:] = power.astype(jnp.int32).astype(jnp.int16)
 
-    def add(idx, ref):
+    def add(idx, ref, pieces=(0, 1)):
         scale = jnp.exp2(ref[:, wide:].astype(jnp.int32).astype(F32) - 16.0)
-        for cols, col in ((slice(0, bins), 0), (slice(bins, wide), BLOCK - 1)):
+        for piece in pieces:
+            cols, col = ((slice(0, bins), 0), (slice(bins, wide), BLOCK - 1))[piece]
             v = ref[:, cols].astype(jnp.int32).astype(F32) + 32768.0
             blk[idx, :, cols] += v * scale[:, col : col + 1]
 
@@ -336,23 +337,32 @@
 
     partial(me)
     x_copy(z).wait_recv()
-    add(me, xr.at[z])
-
     @pl.when(z > 0)
     def _():
         z_copy(z, 1).wait_recv()
-        add(me, zr.at[1, z])
 
     @pl.when(z < 3)
     def _():
         z_copy(z, 0).wait_recv()
-        add(me, zr.at[0, z])
-
+
+    def finish(pieces):
+        add(me, xr.at[z], pieces)
+
+        @pl.when(z > 0)
+        def _():
+            add(me, zr.at[1, z], pieces)
+
+        @pl.when(z < 3)
+        def _():
+            add(me, zr.at[0, z], pieces)
+
+    finish((1,))
     gram[c] = blk[me, :, bins:]
     share = pltpu.make_async_remote_copy(
         gram.at[c], gram.at[c], gs, gr, device_id={"freq": cp}, device_id_type=MESH
     )
     share.start()
+    finish((0,))
     share.wait_recv()
 
     total = jnp.zeros((own, bins), F32)
@@ -440,7 +450,7 @@
             dma((4,)), dma((4,)), dma((4,)), dma((2, 4)), dma(()), dma(()),
         ],
         compiler_params=pltpu.CompilerParams(
-            collective_id=0, has_side_effects=True, vmem_limit_bytes=60 * 1024 * 1024
+            collective_id=0, has_side_effects=True, vmem_limit_bytes=53 * 1024 * 1024
         ),
     )(spectrogram, templates.T, activations, score_mask.T)
     return turned.T, acts

time: 54.2 us -> 54 us (level)
  Pallas kernels: 49.4 us -> 48.5 us
  local copies, waits for them, and re-layouts: 3.93 us -> 4.61 us
    pallas_call x1, Pallas kernels: 49.4 us -> 48.5 us  [fused(): pl.pallas_call(kernel, out_shape=(jax.ShapeDtypeStruct((own, bins), F32),...]
    unnamed x2 -> x6, local copies, waits for them, and re-layouts: 3.93 us -> 4.61 us
where the time goes in v4:
time: 54 us; the launch traced here: 53.8 us
  Pallas kernels  48.5 us (90%)
  local copies, waits for them, and re-layouts  4.61 us (9%)
  between operations  0.65 us (1%)
    pallas_call x1, Pallas kernels, fused(): pl.pallas_call(kernel, out_shape=(jax.ShapeDtypeStruct((own, bins), F32),...  48.5 us
    unnamed x6, local copies, waits for them, and re-layouts  4.61 us

profile of v4, /device:TPU:0, one launch (start us, length us, event | category | flops | bytes accessed | tf_op | source)
XLA Modules:
  0.0 53.8 jit_solution(16971261201780287229)
XLA Ops:
  0.6 0.0 copy-start
  0.6 0.9 %copy-done = f32[1024,64]{0,1:T(8,128)S(1)} copy-done((f32[1024,64]{0,1:T(8,128)S(1)}, f32[1024,64]{0,1:T(8,128)}, u32[]{:S(2)}) %copy-start) | copy-done | bytes 262168
  1.6 0.0 copy-start.1
  1.6 0.7 %copy-done.1 = s32[512,4]{0,1:T(4,128)S(1)} copy-done((s32[512,4]{0,1:T(4,128)S(1)}, s32[512,4]{0,1:T(4,128)}, u32[]{:S(2)}) %copy-start.1) | copy-done | bytes 8216
  2.3 48.5 %shard_map.59 = (f32[64,1024]{1,0:T(8,128)S(1)}, f32[512,512]{1,0:T(8,128)}) custom-call(bf16[1024,512]{1,0:T(8,128)(2,1)} %s_hbm.1, f32[64,1024]{1,0:T(8,128)S(1)} %bitcast.3, f32[512,512]{1,0:T(8,128)} %a_hbm.1, s32[4,512]{1,0:T(4,128)S(1)} %bitcast.5), custom_call_target="tpu_custom_call" | custom-call | tf_op jit(solution)/shard_map/pallas_call | solution.py:421
  50.8 0.7 %copy.8 = f32[1024,64]{0,1:T(8,128)} copy(f32[1024,64]{0,1:T(8,128)S(1)} %bitcast.4) | data formatting | bytes 524288
  51.5 2.3 %copy.9 = f32[512,512]{1,0:T(8,128)} copy(f32[512,512]{1,0:T(8,128)} %get-tuple-element.9) | data formatting | bytes 2097152
Async XLA Ops:
  0.6 1.0 %copy-start = (f32[1024,64]{0,1:T(8,128)S(1)}, f32[1024,64]{0,1:T(8,128)}, u32[]{:S(2)}) copy-start(f32[1024,64]{0,1:T(8,128)} %param.5) | copy-start | bytes 786436
  1.6 0.7 %copy-start.1 = (s32[512,4]{0,1:T(4,128)S(1)}, s32[512,4]{0,1:T(4,128)}, u32[]{:S(2)}) copy-start(s32[512,4]{0,1:T(4,128)} %param.7) | copy-start | bytes 24580
